TPU v7x, 32 devices: a whole 2x2x4 slice. The times are simulated.
32 devices in a mesh: groups: 2 (over y), flat: 4 (over z), dp: 4 (over x, core).
Axes of the slice: x: 2, y: 2, z: 4, core: 2. Of those that a mesh axis runs over, the one named last changes fastest.
Arguments:
- activations: bfloat16 [4096, 14336], P(('groups', 'dp'), 'flat'), parts along dimension 0
- curvature: float32 [4096], P(('groups', 'dp')), parts along dimension 0, may hold values from 0.3 to 3
- vector_now: float32 [28672, 4096], P(('groups', 'flat', 'dp')), parts along dimension 0
- vector_before: float32 [28672, 4096], P(('groups', 'flat', 'dp')), parts along dimension 0, may hold values from -6 to 6
- sign_bits: int32 [28672, 4096], P(('groups', 'flat', 'dp')), parts along dimension 0, may hold values from 0 to 1
- prior_precision: float32 [2], P('groups'), parts along dimension 0, may hold values from 0.2 to 2
- beta_before: float32 [2], P('groups'), parts along dimension 0, may hold values from 0.3 to 1.5
- kept_rows: int32 [8192], P('groups'), parts along dimension 0, may hold values from 0 to 3583
- kept_cols: int32 [8192], P('groups'), parts along dimension 0, may hold values from 0 to 16383
Outputs:
- vector_next: float32 [28672, 4096], P(('groups', 'flat', 'dp')), parts along dimension 0
- alpha_value: float32 [2], P('groups'), parts along dimension 0
- beta_value: float32 [2], P('groups'), parts along dimension 0
- sketch: float32 [8192], P('groups'), parts along dimension 0
There are 2 independent parts, one for each index of `groups`. A program takes and returns all parts, laid end to end along the dimension named above; each array names one. Nothing has to cross between parts.
All inputs are finite; a program needn't handle non-finite values.
Results may differ from a plain program's by a relative error of at most 0.015.
Values may be sent and summed in bfloat16 or wider, within the bound.
A program may use at most 256 MiB of HBM per device.

v0:
```python
import math
import jax
import jax.numpy as jnp
from jax import lax
from jax.sharding import PartitionSpec as P

BLOCK = 128


def parity_sign(row_index, col_index):
    common_bits = jnp.bitwise_and(row_index, col_index)
    parity_sum = jnp.zeros_like(common_bits)
    for position in range(BLOCK.bit_length() - 1):
        parity_sum = parity_sum + jnp.bitwise_and(jnp.right_shift(common_bits, position), 1)
    return (1 - 2 * jnp.bitwise_and(parity_sum, 1)).astype(jnp.float32) / math.sqrt(BLOCK)


def hadamard_table():
    row_index = lax.broadcasted_iota(jnp.int32, (BLOCK, BLOCK), 0)
    col_index = lax.broadcasted_iota(jnp.int32, (BLOCK, BLOCK), 1)
    return parity_sign(row_index, col_index)


def pick_dense(column_block, hadamard, own_index, kept_rows, kept_cols):
    cols_here = column_block.shape[1]
    section_two = jnp.einsum(
        "ri,bic->brc",
        hadamard,
        column_block.reshape(-1, BLOCK, cols_here),
        precision=lax.Precision.HIGHEST,
    )
    section_two = section_two.reshape(-1, cols_here)
    first_col = own_index * cols_here
    inside = jnp.logical_and(kept_cols >= first_col, kept_cols < first_col + cols_here)
    local_col = jnp.clip(kept_cols - first_col, 0, cols_here - 1)
    return jnp.where(inside, section_two[kept_rows, local_col], 0.0)


def on_device(
    activations,
    curvature,
    vector_now,
    vector_before,
    sign_bits,
    prior_precision,
    beta_before,
    kept_rows,
    kept_cols,
):
    token_count = activations.shape[0]
    out_width = vector_now.shape[1]
    local_rows = vector_now.shape[0]
    flat_count = lax.axis_size("flat")
    data_count = lax.axis_size("dp")
    total_tokens = token_count * data_count
    total_cells = local_rows * out_width * flat_count * data_count
    vector_half = vector_now.astype(jnp.bfloat16)
    columns = activations
    partial_out = jnp.dot(
        columns,
        lax.all_gather(vector_half, "dp", axis=0, tiled=True),
        preferred_element_type=jnp.float32,
    )
    shares = lax.psum_scatter(
        partial_out.astype(jnp.bfloat16), "flat", scatter_dimension=1, tiled=True
    ).astype(jnp.float32)
    scaled_share = (curvature[:, None] * shares / total_tokens).astype(jnp.bfloat16)
    scaled = lax.all_gather(scaled_share, "flat", axis=1, tiled=True)
    columns = activations
    image_data = lax.psum_scatter(
        lax.dot_general(
            columns, scaled, (((0,), (0,)), ((), ())), preferred_element_type=jnp.float32
        ).astype(jnp.bfloat16),
        "dp",
        scatter_dimension=0,
        tiled=True,
    ).astype(jnp.float32)
    new_image = image_data + prior_precision[0] * vector_now
    beta_old = beta_before[0]
    alpha_value = lax.psum(jnp.sum(new_image * vector_now), ("flat", "dp")) / total_cells
    residual = new_image - alpha_value * vector_now - beta_old * vector_before
    square = lax.psum(jnp.sum(residual * residual), ("flat", "dp")) / total_cells
    beta_value = jnp.sqrt(square + 1e-06)
    vector_next = residual / beta_value
    hadamard = hadamard_table()
    signed = (2 * sign_bits - 1).astype(jnp.float32) * vector_next
    rows_here = local_rows * out_width // (BLOCK * BLOCK)
    section_one = jnp.dot(signed.reshape(-1, BLOCK), hadamard, precision=lax.Precision.HIGHEST)
    section_one = section_one.reshape(rows_here, BLOCK * BLOCK)
    own_index = lax.axis_index(("flat", "dp"))
    column_block = lax.all_to_all(
        section_one.astype(jnp.bfloat16), ("flat", "dp"), split_axis=1, concat_axis=0, tiled=True
    ).astype(section_one.dtype)
    local_values = pick_dense(column_block, hadamard, own_index, kept_rows, kept_cols)
    sketch = lax.psum(local_values, ("flat", "dp"))
    return (vector_next, alpha_value.reshape(1), beta_value.reshape(1), sketch)


def solution(mesh):
    placed = (
        P(("groups", "dp"), "flat"),
        P(("groups", "dp")),
        P(("groups", "flat", "dp"), None),
        P(("groups", "flat", "dp"), None),
        P(("groups", "flat", "dp"), None),
        P("groups"),
        P("groups"),
        P("groups"),
        P("groups"),
    )
    return jax.shard_map(
        on_device,
        mesh=mesh,
        in_specs=placed,
        out_specs=(P(("groups", "flat", "dp"), None), P("groups"), P("groups"), P("groups")),
        check_vma=False,
    )
```

profile of v0, /device:TPU:0, one launch (start us, length us, event | category | flops | bytes accessed | tf_op | source)
XLA Modules:
  0.0 1159.3 jit_solution(15920801584408900253)
XLA Ops:
  7.2 9.4 convert_element_type.37
  16.6 0.0 reduce-scatter.5.cloned.1.call-start
  16.7 180.8 %all-gather.3.cloned.1.call-done = bf16[3584,4096]{1,0:T(8,128)(2,1)} async-done(((bf16[896,4096]{1,0:T(8,128)(2,1)}), bf16[3584,4096]{1,0:T(8,128)(2,1)}) %all-gather.3.cloned.1.call-update) | async-done | bytes 29360144 | tf_op jit(solution)/shard_map/all_gather | solution.py:61
  197.4 23.0 %convolution_convert_fusion.2 = bf16[512,4096]{1,0:T(8,128)(2,1)} fusion(bf16[512,3584]{1,0:T(8,128)(2,1)} %param.9, bf16[3584,4096]{1,0:T(8,128)(2,1)} %all-gather.3.cloned.1.call-done), kind=kOutput, calls=%fused_computation.10 | convolution fusion | flops 15034482688 | bytes 37224448 | tf_op jit(solution)/shard_map/dot_general | solution.py:59
  220.5 0.0 all-gather.5.cloned.1.call-start
  220.5 76.9 %reduce-scatter.5.cloned.1.call-done = bf16[512,1024]{1,0:T(8,128)(2,1)} async-done(((bf16[512,4096]{1,0:T(8,128)(2,1)}), bf16[512,1024]{1,0:T(8,128)(2,1)}) %reduce-scatter.5.cloned.1.call-update) | async-done | bytes 1048592 | tf_op jit(solution)/shard_map/reduce_scatter | solution.py:64
  297.4 2.5 multiply_convert_fusion
  299.9 0.2 reduce-scatter.7.cloned.1.call-start
  300.2 81.2 %all-gather.5.cloned.1.call-done = bf16[512,4096]{1,0:T(8,128)(2,1)} async-done(((bf16[512,1024]{1,0:T(8,128)(2,1)}), bf16[512,4096]{1,0:T(8,128)(2,1)}) %all-gather.5.cloned.1.call-update) | async-done | bytes 4194320 | tf_op jit(solution)/shard_map/all_gather | solution.py:68
  381.4 22.3 %fusion = bf16[3584,4096]{0,1:T(8,128)(2,1)} fusion(bf16[512,4096]{1,0:T(8,128)(2,1)} %all-gather.5.cloned.1.call-done, bf16[512,3584]{1,0:T(8,128)(2,1)} %param.9), kind=kOutput, calls=%fused_computation.3 | convolution fusion | flops 15047065600 | bytes 37224448 | tf_op jit(solution)/shard_map/dot_general | solution.py:71
  403.7 37.0 %copy.36 = bf16[3584,4096]{1,0:T(8,128)(2,1)} copy(bf16[3584,4096]{0,1:T(8,128)(2,1)} %fusion) | data formatting | bytes 58720256
  440.7 16.7 %copy.28 = f32[896,4096]{0,1:T(8,128)} copy(f32[896,4096]{1,0:T(8,128)} %param.11) | data formatting | bytes 29360128 | tf_op args[2]
  458.1 18.0 %copy.31 = f32[896,4096]{0,1:T(8,128)} copy(f32[896,4096]{1,0:T(8,128)} %param.12) | data formatting | bytes 29360128 | tf_op args[3]
  476.1 171.1 %reduce-scatter.7.cloned.1.call-done = bf16[896,4096]{1,0:T(8,128)(2,1)} async-done(((bf16[3584,4096]{1,0:T(8,128)(2,1)}), bf16[896,4096]{1,0:T(8,128)(2,1)}) %reduce-scatter.7.cloned.1.call-update) | async-done | bytes 7340048
  647.2 10.8 copy.37
  658.1 11.6 %multiply_reduce_fusion.1 = f32[]{:T(128)} fusion(f32[896,4096]{0,1:T(8,128)} %copy.28, bf16[896,4096]{0,1:T(8,128)(2,1)} %copy.37, f32[]{:T(128)} %bitcast.22), kind=kLoop, calls=%fused_computation.7 | loop fusion | flops 18350080 | bytes 22020104 | tf_op jit(solution)/shard_map/reduce_sum | solution.py:80
  670.4 32.9 %psum.21 = f32[]{:T(128)} all-reduce(f32[]{:T(128)} %multiply_reduce_fusion.1), channel_id=1, replica_groups=mesh['groups'=2,'flat'=4,'dp'=4] {'flat','dp'}, use_global_device_ids=true, to_apply=%region_3.0 | all-reduce | flops 1 | bytes 8 | tf_op jit(solution)/shard_map/psum | solution.py:80
  703.9 13.4 %multiply_reduce_fusion = f32[]{:T(128)} fusion(f32[896,4096]{0,1:T(8,128)} %copy.31, f32[]{:T(128)} %bitcast.25, f32[896,4096]{0,1:T(8,128)} %copy.28, f32[]{:T(128)} %div.28, f32[]{:T(128)} %bitcast.23, bf16[896,4096]{0,1:T(8,128)(2,1)} %copy.37), kind=kLoop, calls=%fused_computation.5 | loop fusion | flops 33030144 | bytes 36700176 | tf_op jit(solution)/shard_map/reduce_sum | solution.py:82
  717.3 16.1 %copy.32 = s32[896,4096]{0,1:T(8,128)} copy(s32[896,4096]{1,0:T(8,128)} %param.13) | data formatting | bytes 29360128 | tf_op args[4]
  733.4 30.3 %psum.22 = f32[]{:T(128)} all-reduce(f32[]{:T(128)} %multiply_reduce_fusion), channel_id=1, replica_groups=mesh['groups'=2,'flat'=4,'dp'=4] {'flat','dp'}, use_global_device_ids=true, to_apply=%region_5.0 | all-reduce | flops 1 | bytes 8 | tf_op jit(solution)/shard_map/psum | solution.py:82
  764.4 28.3 %convert_multiply_fusion = (f32[896,4096]{0,1:T(8,128)}, f32[896,4096]{0,1:T(8,128)}) fusion(s32[896,4096]{0,1:T(8,128)} %copy.32, f32[]{:T(128)} %sqrt.3, f32[896,4096]{0,1:T(8,128)} %copy.31, f32[]{:T(128)} %bitcast.26, f32[896,4096]{0,1:T(8,128)} %copy.28, f32[]{:T(128)} %div.28, f32[]{:T(128)} %bitcast.24, bf16[896,4096]{0,1:T(8,128)(2,1)} %copy.37), kind=kLoop, calls=%fused_computation.4 | loop fusion | flops 44040192 | bytes 80740368 | tf_op jit(solution)/shard_map/mul | solution.py:86
  792.7 16.1 %copy.33 = f32[896,4096]{1,0:T(8,128)} copy(f32[896,4096]{0,1:T(8,128)} %get-tuple-element.16) | data formatting | bytes 29360128 | tf_op jit(solution)/shard_map/mul | solution.py:86
  808.8 15.8 %reshape.33 = f32[28672,128]{1,0:T(8,128)} reshape(f32[896,4096]{1,0:T(8,128)} %copy.33) | data formatting | bytes 29360128 | tf_op jit(solution)/shard_map/reshape | solution.py:88
  824.6 15.6 %convolution_convert_fusion = bf16[28672,128]{1,0:T(8,128)(2,1)} fusion(f32[28672,128]{1,0:T(8,128)} %reshape.33), kind=kOutput, calls=%fused_computation.1 | convolution fusion | flops 5641240576 | bytes 22020096 | tf_op jit(solution)/shard_map/dot_general | solution.py:88
  840.3 11.8 %convert_element_type.47 = bf16[224,16,1024]{2,1,0:T(8,128)(2,1)} reshape(bf16[28672,128]{1,0:T(8,128)(2,1)} %convolution_convert_fusion) | data formatting | bytes 14680064 | tf_op jit(solution)/shard_map/convert_element_type | solution.py:92
  852.0 10.2 copy.34
  862.2 5.0 all-to-all-start
  867.2 16.1 %copy.35 = f32[896,4096]{1,0:T(8,128)} copy(f32[896,4096]{0,1:T(8,128)} %get-tuple-element.17) | data formatting | bytes 29360128
  883.3 116.0 %all-to-all-done = bf16[224,16,1024]{2,0,1:T(8,128)(2,1)} async-done(((bf16[224,16,1024]{2,0,1:T(8,128)(2,1)}), bf16[224,16,1024]{2,0,1:T(8,128)(2,1)}, u32[]{:S(2)}, u32[]{:S(2)}) %all-to-all-start) | async-done | bytes 7340064 | tf_op jit(solution)/shard_map/all_to_all | solution.py:91
  999.3 12.7 %fusion.1 = f32[28,1024,128]{1,2,0:T(8,128)} fusion(bf16[28,128,1024]{2,1,0:T(8,128)(2,1)} %bitcast.6), kind=kOutput, calls=%fused_computation.12 | convolution fusion | flops 5637570560 | bytes 22020096 | tf_op jit(solution)/shard_map/ri,bic->brc/dot_general | solution.py:26
  1012.0 50.1 %gather_fusion = f32[4096]{0:T(1024)S(1)} fusion(f32[3584,1024]{1,0:T(8,128)} %bitcast.27, s32[4096]{0:T(1024)S(1)} %fusion.5), kind=kCustom, calls=%fused_computation | custom fusion | bytes 65536 | tf_op jit(solution)/shard_map/gather | solution.py:36
  1062.1 88.3 %psum.23 = f32[4096]{0:T(1024)} all-reduce(f32[4096]{0:T(1024)S(1)} %and_select_fusion), channel_id=1, replica_groups=mesh['groups'=2,'flat'=4,'dp'=4] {'flat','dp'}, use_global_device_ids=true, to_apply=%region_6.7 | all-reduce | flops 4096 | bytes 32768 | tf_op jit(solution)/shard_map/psum | solution.py:95
  (13 shorter events, 0.1 us)
Async XLA Ops:
  7.2 190.3 %all-gather.3.cloned.1.call-start = ((), (), s32[]{:S(2)}) async-start(), calls=%async_computation.3 | async-start | bytes 36700160 | tf_op jit(solution)/shard_map/all_gather | solution.py:61
  16.6 280.8 %copy-start.2 = (f32[512]{0:T(512)S(1)}, f32[512]{0:T(512)}, u32[]{:S(2)}) copy-start(f32[512]{0:T(512)} %param.10) | copy-start | bytes 6148
  16.6 280.8 %reduce-scatter.5.cloned.1.call-start = ((), (), s32[]{:S(2)}) async-start(), calls=%async_computation.4 | async-start | bytes 5242880 | tf_op jit(solution)/shard_map/reduce_scatter | solution.py:64
  220.5 160.9 %all-gather.5.cloned.1.call-start = ((), (), s32[]{:S(2)}) async-start(), calls=%async_computation.5 | async-start | bytes 5242880 | tf_op jit(solution)/shard_map/all_gather | solution.py:68
  299.9 347.3 %reduce-scatter.7.cloned.1.call-start = ((), (), s32[]{:S(2)}) async-start(), calls=%async_computation.6 | async-start | bytes 36700160
  852.0 15.2 %copy-start = (s32[4096]{0:T(1024)S(1)}, s32[4096]{0:T(1024)}, u32[]{:S(2)}) copy-start(s32[4096]{0:T(1024)} %param.17) | copy-start | bytes 49156
  852.0 15.2 %copy-start.1 = (s32[4096]{0:T(1024)S(1)}, s32[4096]{0:T(1024)}, u32[]{:S(2)}) copy-start(s32[4096]{0:T(1024)} %param.16) | copy-start | bytes 49156
  862.2 137.1 %all-to-all-start = ((bf16[224,16,1024]{2,0,1:T(8,128)(2,1)}), bf16[224,16,1024]{2,0,1:T(8,128)(2,1)}, u32[]{:S(2)}, u32[]{:S(2)}) async-start(bf16[224,16,1024]{2,0,1:T(8,128)(2,1)} %copy.34), calls=%async_computation.1 | async-start | bytes 14680064 | tf_op jit(solution)/shard_map/all_to_all | solution.py:91
Sparse Core Ops, SparseCore 0:
  16.7 180.6 all-gather.2
  220.6 76.7 reduce-scatter.4
  300.1 81.2 all-gather.4
  440.8 206.3 reduce-scatter.6
where the time goes:
time: 1160 us
  waiting for transfers between devices  626 us (54%)
  local copies, waits for them, and re-layouts  219 us (19%)
  blocking collectives  152 us (13%)
  matrix products  73.6 us (6%)
  other arithmetic  65.2 us (6%)
  between operations  18.8 us (2%)
    all_gather x1, waiting for transfers between devices, on_device(): lax.all_gather(vector_half, 'dp', axis=0, tiled=True)  181 us
    unnamed x5, waiting for transfers between devices  171 us
    all_to_all x1, waiting for transfers between devices, on_device(): lax.all_to_all(section_one.astype(jnp.bfloat16), ('flat', 'dp'), split_ax...  116 us
    unnamed x12, local copies, waits for them, and re-layouts  115 us
    psum x1, blocking collectives, on_device(): sketch = lax.psum(local_values, ('flat', 'dp'))  88.3 us
    all_gather x1, waiting for transfers between devices, on_device(): scaled = lax.all_gather(scaled_share, 'flat', axis=1, tiled=True)  81.2 us
    reduce_scatter x1, waiting for transfers between devices, on_device(): lax.psum_scatter(partial_out.astype(jnp.bfloat16), 'flat', scatter_dimens...  76.9 us
    gather x1, local copies, waits for them, and re-layouts, pick_dense(): return jnp.where(inside, section_two[kept_rows, local_col], 0.0)  50.1 us
  transfers between devices with their start and end apart: 5, of which 5 were waited for; matrix products, arithmetic and copies ran while one was open for 4% of the time, Pallas kernels for 0%

commit v1 on v0

--- a/solution.py
+++ b/solution.py
@@ -5,6 +5,20 @@
 from jax.sharding import PartitionSpec as P
 
 BLOCK = 128
+
+
+def _recast_sections(mine, in_dim, a0):
+    w1 = mine.shape
+    step_out = mine.reshape(*w1[:in_dim], a0, w1[in_dim] // a0, *w1[in_dim + 1 :])
+    response = jnp.moveaxis(step_out, in_dim, 0)
+    return response
+
+
+def series_save(t0, d0):
+    after = list(t0.shape[1:])
+    after[d0] *= t0.shape[0]
+    tmp = jnp.moveaxis(t0, 0, d0).reshape(after)
+    return tmp
 
 
 def parity_sign(row_index, col_index):
@@ -47,6 +61,18 @@
     kept_rows,
     kept_cols,
 ):
+
+    def take_the_zone(v0, across, u_in, payload):
+        x_now, kept_arr = (lax.psum(1, across), lax.axis_index(across))
+        o_now = _recast_sections(v0, u_in, x_now)
+        lanes = [o_now[kept_arr]]
+        for t in range(1, x_now):
+            current_arr = o_now[kept_arr ^ t]
+            lanes.append(lax.ppermute(current_arr, across, [(rr, rr ^ t) for rr in range(x_now)]))
+        o_now = jnp.stack(lanes, 0)[kept_arr ^ jnp.arange(x_now)]
+        low = series_save(o_now, payload)
+        return low
+
     token_count = activations.shape[0]
     out_width = vector_now.shape[1]
     local_rows = vector_now.shape[0]
@@ -88,8 +114,8 @@
     section_one = jnp.dot(signed.reshape(-1, BLOCK), hadamard, precision=lax.Precision.HIGHEST)
     section_one = section_one.reshape(rows_here, BLOCK * BLOCK)
     own_index = lax.axis_index(("flat", "dp"))
-    column_block = lax.all_to_all(
-        section_one.astype(jnp.bfloat16), ("flat", "dp"), split_axis=1, concat_axis=0, tiled=True
+    column_block = take_the_zone(
+        section_one.astype(jnp.bfloat16), ("flat", "dp"), 1, payload=0
     ).astype(section_one.dtype)
     local_values = pick_dense(column_block, hadamard, own_index, kept_rows, kept_cols)
     sketch = lax.psum(local_values, ("flat", "dp"))

time: 1160 us -> 1220 us (1.052); the launches traced: 1160 us -> 1210 us
  local copies, waits for them, and re-layouts: 219 us -> 286 us
  waiting for transfers between devices: 626 us -> 598 us
    all_to_all x1 -> x0, waiting for transfers between devices: 116 us -> none  [on_device(): lax.all_to_all(section_one.astype(jnp.bfloat16), ('flat', 'dp'), split_ax...]
    ppermute x0 -> x15, waiting for transfers between devices: none -> 105 us  [take_the_zone(): lax.ppermute(current_arr, across, [(rr, rr ^ t) for rr in range(x_now)])]
    unnamed x12 -> x60, local copies, waits for them, and re-layouts: 115 us -> 153 us
    another operation x0 -> x2, local copies, waits for them, and re-layouts: none -> 32.5 us
    unnamed x5, waiting for transfers between devices: 171 us -> 154 us
    ppermute x0 -> x15, starting transfers between devices: none -> 13.2 us  [take_the_zone(): lax.ppermute(current_arr, across, [(rr, rr ^ t) for rr in range(x_now)])]
  transfers between devices with their start and end apart: 5 -> 19, of which waited for: 5 -> 10; matrix products, arithmetic and copies ran while one was open for 4% -> 8% of each run, Pallas kernels for 0% -> 0%
where the time goes in v1:
time: 1220 us; the launch traced here: 1210 us
  waiting for transfers between devices  598 us (49%)
  local copies, waits for them, and re-layouts  286 us (23%)
  blocking collectives  151 us (12%)
  matrix products  73.6 us (6%)
  other arithmetic  65.3 us (5%)
  between operations  19.1 us (2%)
  starting transfers between devices  13.9 us (1%)
    all_gather x1, waiting for transfers between devices, on_device(): lax.all_gather(vector_half, 'dp', axis=0, tiled=True)  181 us
    unnamed x5, waiting for transfers between devices  154 us
    unnamed x60, local copies, waits for them, and re-layouts  153 us
    ppermute x15, waiting for transfers between devices, take_the_zone(): lax.ppermute(current_arr, across, [(rr, rr ^ t) for rr in range(x_now)])  105 us
    psum x1, blocking collectives, on_device(): sketch = lax.psum(local_values, ('flat', 'dp'))  87.6 us
    all_gather x1, waiting for transfers between devices, on_device(): scaled = lax.all_gather(scaled_share, 'flat', axis=1, tiled=True)  80.9 us
    reduce_scatter x1, waiting for transfers between devices, on_device(): lax.psum_scatter(partial_out.astype(jnp.bfloat16), 'flat', scatter_dimens...  76.9 us
    gather x1, local copies, waits for them, and re-layouts, pick_dense(): return jnp.where(inside, section_two[kept_rows, local_col], 0.0)  50.2 us
  transfers between devices with their start and end apart: 19, of which 10 were waited for; matrix products, arithmetic and copies ran while one was open for 8% of the time, Pallas kernels for 0%

profile of v1, /device:TPU:0, one launch (start us, length us, event | category | flops | bytes accessed | tf_op | source)
XLA Modules:
  0.0 1207.1 jit_solution(17791406460063337471)
XLA Ops:
  7.2 9.4 convert_element_type.37
  16.7 180.8 %all-gather.3.cloned.1.call-done = bf16[3584,4096]{1,0:T(8,128)(2,1)} async-done(((bf16[896,4096]{1,0:T(8,128)(2,1)}), bf16[3584,4096]{1,0:T(8,128)(2,1)}) %all-gather.3.cloned.1.call-update) | async-done | bytes 29360144 | tf_op jit(solution)/shard_map/all_gather | solution.py:87
  197.4 23.0 %convolution_convert_fusion.2 = bf16[512,4096]{1,0:T(8,128)(2,1)} fusion(bf16[512,3584]{1,0:T(8,128)(2,1)} %param.9, bf16[3584,4096]{1,0:T(8,128)(2,1)} %all-gather.3.cloned.1.call-done), kind=kOutput, calls=%fused_computation.11 | convolution fusion | flops 15034482688 | bytes 37224448 | tf_op jit(solution)/shard_map/dot_general | solution.py:85
  220.5 76.9 %reduce-scatter.5.cloned.1.call-done = bf16[512,1024]{1,0:T(8,128)(2,1)} async-done(((bf16[512,4096]{1,0:T(8,128)(2,1)}), bf16[512,1024]{1,0:T(8,128)(2,1)}) %reduce-scatter.5.cloned.1.call-update) | async-done | bytes 1048592 | tf_op jit(solution)/shard_map/reduce_scatter | solution.py:90
  300.4 80.9 %all-gather.5.cloned.1.call-done = bf16[512,4096]{1,0:T(8,128)(2,1)} async-done(((bf16[512,1024]{1,0:T(8,128)(2,1)}), bf16[512,4096]{1,0:T(8,128)(2,1)}) %all-gather.5.cloned.1.call-update) | async-done | bytes 4194320 | tf_op jit(solution)/shard_map/all_gather | solution.py:94
  381.4 22.3 %fusion = bf16[3584,4096]{0,1:T(8,128)(2,1)} fusion(bf16[512,4096]{1,0:T(8,128)(2,1)} %all-gather.5.cloned.1.call-done, bf16[512,3584]{1,0:T(8,128)(2,1)} %param.9), kind=kOutput, calls=%fused_computation.4 | convolution fusion | flops 15047065600 | bytes 37224448 | tf_op jit(solution)/shard_map/dot_general | solution.py:97
  403.7 39.6 %copy.65 = bf16[3584,4096]{1,0:T(8,128)(2,1)} copy(bf16[3584,4096]{0,1:T(8,128)(2,1)} %fusion) | data formatting | bytes 58720256
  443.4 16.6 %copy.42 = f32[896,4096]{0,1:T(8,128)} copy(f32[896,4096]{1,0:T(8,128)} %param.11) | data formatting | bytes 29360128 | tf_op args[2]
  460.6 18.0 %copy.45 = f32[896,4096]{0,1:T(8,128)} copy(f32[896,4096]{1,0:T(8,128)} %param.12) | data formatting | bytes 29360128 | tf_op args[3]
  479.3 16.3 %copy.46 = s32[896,4096]{0,1:T(8,128)} copy(s32[896,4096]{1,0:T(8,128)} %param.13) | data formatting | bytes 29360128 | tf_op args[4]
  495.6 154.3 %reduce-scatter.7.cloned.1.call-done = bf16[896,4096]{1,0:T(8,128)(2,1)} async-done(((bf16[3584,4096]{1,0:T(8,128)(2,1)}), bf16[896,4096]{1,0:T(8,128)(2,1)}) %reduce-scatter.7.cloned.1.call-update) | async-done | bytes 7340048
  649.9 10.7 copy.66
  660.6 11.6 multiply_reduce_fusion.1
  672.3 32.9 %psum.21 = f32[]{:T(128)} all-reduce(f32[]{:T(128)} %multiply_reduce_fusion.1), channel_id=1, replica_groups=mesh['groups'=2,'flat'=4,'dp'=4] {'flat','dp'}, use_global_device_ids=true, to_apply=%region_3.0 | all-reduce | flops 1 | bytes 8 | tf_op jit(solution)/shard_map/psum | solution.py:106
  705.8 13.4 %multiply_reduce_fusion = f32[]{:T(128)} fusion(f32[896,4096]{0,1:T(8,128)} %copy.45, f32[]{:T(128)} %bitcast.104, f32[896,4096]{0,1:T(8,128)} %copy.42, f32[]{:T(128)} %div.28, f32[]{:T(128)} %bitcast.102, bf16[896,4096]{0,1:T(8,128)(2,1)} %copy.66), kind=kLoop, calls=%fused_computation.6 | loop fusion | flops 33030144 | bytes 36700176 | tf_op jit(solution)/shard_map/reduce_sum | solution.py:108
  719.2 30.3 %psum.22 = f32[]{:T(128)} all-reduce(f32[]{:T(128)} %multiply_reduce_fusion), channel_id=1, replica_groups=mesh['groups'=2,'flat'=4,'dp'=4] {'flat','dp'}, use_global_device_ids=true, to_apply=%region_5.0 | all-reduce | flops 1 | bytes 8 | tf_op jit(solution)/shard_map/psum | solution.py:108
  750.2 28.3 %convert_multiply_fusion = (f32[896,4096]{0,1:T(8,128)}, f32[896,4096]{0,1:T(8,128)}) fusion(s32[896,4096]{0,1:T(8,128)} %copy.46, f32[]{:T(128)} %sqrt.3, f32[896,4096]{0,1:T(8,128)} %copy.45, f32[]{:T(128)} %bitcast.105, f32[896,4096]{0,1:T(8,128)} %copy.42, f32[]{:T(128)} %div.28, f32[]{:T(128)} %bitcast.103, bf16[896,4096]{0,1:T(8,128)(2,1)} %copy.66), kind=kLoop, calls=%fused_computation.5 | loop fusion | flops 44040192 | bytes 80740368 | tf_op jit(solution)/shard_map/mul | solution.py:112
  778.5 16.1 %copy.47 = f32[896,4096]{1,0:T(8,128)} copy(f32[896,4096]{0,1:T(8,128)} %get-tuple-element.16) | data formatting | bytes 29360128 | tf_op jit(solution)/shard_map/mul | solution.py:112
  794.6 15.8 %reshape.79 = f32[28672,128]{1,0:T(8,128)} reshape(f32[896,4096]{1,0:T(8,128)} %copy.47) | data formatting | bytes 29360128 | tf_op jit(solution)/shard_map/reshape | solution.py:114
  810.4 15.6 %convolution_convert_fusion = bf16[28672,128]{1,0:T(8,128)(2,1)} fusion(f32[28672,128]{1,0:T(8,128)} %reshape.79), kind=kOutput, calls=%fused_computation.2 | convolution fusion | flops 5641240576 | bytes 22020096 | tf_op jit(solution)/shard_map/dot_general | solution.py:114
  826.0 11.8 convert_element_type.47
  837.7 31.7 %constant_dynamic-slice_fusion = (bf16[224,1,1024]{2,1,0:T(2,128)(2,1)S(1)}, bf16[224,1,1024]{2,1,0:T(2,128)(2,1)S(1)}, bf16[224,1,1024]{2,1,0:T(2,128)(2,1)S(1)...) fusion(bf16[224,16,1024]{2,1,0:T(8,128)(2,1)} %convert_element_, ...), kind=kLoop, calls=%fused_computation.58 | loop fusion | bytes 14680128 | tf_op jit(solution)/shard_map/dynamic-slice.15
  892.3 16.1 %copy.64 = f32[896,4096]{1,0:T(8,128)} copy(f32[896,4096]{0,1:T(8,128)} %get-tuple-element.17) | data formatting | bytes 29360128
  922.9 11.6 collective-permute-done.5
  935.8 7.7 collective-permute-done.6
  947.7 36.6 %collective-permute-done.7 = bf16[224,1024]{1,0:T(8,128)(2,1)S(1)} collective-permute-done((bf16[224,1024]{1,0:T(8,128)(2,1)}, bf16[224,1024]{1,0:T(8,128)(2,1)S(1)}, u32[]{:S(2)}, u32[]{:S(2)}) %collective-permute-start.7) | collective-permute-done | bytes 458784 | tf_op jit(solution)/shard_map/ppermute | solution.py:71
  985.1 12.7 %collective-permute-done.8 = bf16[224,1024]{1,0:T(8,128)(2,1)S(1)} collective-permute-done((bf16[224,1024]{1,0:T(8,128)(2,1)}, bf16[224,1024]{1,0:T(8,128)(2,1)S(1)}, u32[]{:S(2)}, u32[]{:S(2)}) %collective-permute-start.8) | collective-permute-done | bytes 458784 | tf_op jit(solution)/shard_map/ppermute | solution.py:71
  998.6 19.9 %collective-permute-done.9 = bf16[224,1024]{1,0:T(8,128)(2,1)S(1)} collective-permute-done((bf16[224,1024]{1,0:T(8,128)(2,1)}, bf16[224,1024]{1,0:T(8,128)(2,1)S(1)}, u32[]{:S(2)}, u32[]{:S(2)}) %collective-permute-start.9) | collective-permute-done | bytes 458784 | tf_op jit(solution)/shard_map/ppermute | solution.py:71
  1019.6 16.8 %collective-permute-done.10 = bf16[224,1024]{1,0:T(8,128)(2,1)S(1)} collective-permute-done((bf16[224,1024]{1,0:T(8,128)(2,1)}, bf16[224,1024]{1,0:T(8,128)(2,1)S(1)}, u32[]{:S(2)}, u32[]{:S(2)}) %collective-permute-start.10) | collective-permute-done | bytes 458784 | tf_op jit(solution)/shard_map/ppermute | solution.py:71
  1047.5 12.7 %fusion.2 = f32[28,1024,128]{1,2,0:T(8,128)} fusion(bf16[28,128,1024]{2,1,0:T(8,128)(2,1)} %bitcast.107), kind=kOutput, calls=%fused_computation.45 | convolution fusion | flops 5637570560 | bytes 22020096 | tf_op jit(solution)/shard_map/ri,bic->brc/dot_general | solution.py:40
  1060.2 50.2 %gather_fusion.1 = f32[4096]{0:T(1024)S(1)} fusion(f32[3584,1024]{1,0:T(8,128)} %bitcast.106, s32[4096]{0:T(1024)S(1)} %fusion.6), kind=kCustom, calls=%fused_computation.1 | custom fusion | bytes 65536 | tf_op jit(solution)/shard_map/gather | solution.py:50
  1110.5 87.6 %psum.23 = f32[4096]{0:T(1024)} all-reduce(f32[4096]{0:T(1024)S(1)} %and_select_fusion), channel_id=1, replica_groups=mesh['groups'=2,'flat'=4,'dp'=4] {'flat','dp'}, use_global_device_ids=true, to_apply=%region_6.7 | all-reduce | flops 4096 | bytes 32768 | tf_op jit(solution)/shard_map/psum | solution.py:121
  (93 shorter events, 60.0 us)
Async XLA Ops:
  7.2 190.3 %all-gather.3.cloned.1.call-start = ((), (), s32[]{:S(2)}) async-start(), calls=%async_computation.2 | async-start | bytes 36700160 | tf_op jit(solution)/shard_map/all_gather | solution.py:87
  16.6 280.8 %copy-start.11 = (f32[512]{0:T(512)S(1)}, f32[512]{0:T(512)}, u32[]{:S(2)}) copy-start(f32[512]{0:T(512)} %param.10) | copy-start | bytes 6148
  16.6 280.8 %reduce-scatter.5.cloned.1.call-start = ((), (), s32[]{:S(2)}) async-start(), calls=%async_computation.3 | async-start | bytes 5242880 | tf_op jit(solution)/shard_map/reduce_scatter | solution.py:90
  220.5 160.9 %all-gather.5.cloned.1.call-start = ((), (), s32[]{:S(2)}) async-start(), calls=%async_computation.4 | async-start | bytes 5242880 | tf_op jit(solution)/shard_map/all_gather | solution.py:94
  299.9 350.0 %reduce-scatter.7.cloned.1.call-start = ((), (), s32[]{:S(2)}) async-start(), calls=%async_computation.5 | async-start | bytes 36700160
  837.7 34.0 %copy-start.9 = (s32[4096]{0:T(1024)S(1)}, s32[4096]{0:T(1024)}, u32[]{:S(2)}) copy-start(s32[4096]{0:T(1024)} %param.17) | copy-start | bytes 49156
  837.7 34.0 %copy-start.10 = (s32[4096]{0:T(1024)S(1)}, s32[4096]{0:T(1024)}, u32[]{:S(2)}) copy-start(s32[4096]{0:T(1024)} %param.16) | copy-start | bytes 49156
  869.4 14.3 %copy-start.6 = (bf16[224,1,1024]{2,1,0:T(2,128)(2,1)S(1)}, bf16[224,1,1024]{2,1,0:T(2,128)(2,1)}, u32[]{:S(2)}) copy-start(bf16[224,1,1024]{2,1,0:T(2,128)(2,1)} %get-tuple-element.27) | copy-start | bytes 1376260
  869.4 15.3 %copy-start.5 = (bf16[224,1,1024]{2,1,0:T(2,128)(2,1)S(1)}, bf16[224,1,1024]{2,1,0:T(2,128)(2,1)}, u32[]{:S(2)}) copy-start(bf16[224,1,1024]{2,1,0:T(2,128)(2,1)} %get-tuple-element.26) | copy-start | bytes 1376260
  869.4 16.2 %copy-start.4 = (bf16[224,1,1024]{2,1,0:T(2,128)(2,1)S(1)}, bf16[224,1,1024]{2,1,0:T(2,128)(2,1)}, u32[]{:S(2)}) copy-start(bf16[224,1,1024]{2,1,0:T(2,128)(2,1)} %get-tuple-element.25) | copy-start | bytes 1376260
  869.4 17.1 %copy-start.3 = (bf16[224,1,1024]{2,1,0:T(2,128)(2,1)S(1)}, bf16[224,1,1024]{2,1,0:T(2,128)(2,1)}, u32[]{:S(2)}) copy-start(bf16[224,1,1024]{2,1,0:T(2,128)(2,1)} %get-tuple-element.24) | copy-start | bytes 1376260
  869.4 18.0 %copy-start.2 = (bf16[224,1,1024]{2,1,0:T(2,128)(2,1)S(1)}, bf16[224,1,1024]{2,1,0:T(2,128)(2,1)}, u32[]{:S(2)}) copy-start(bf16[224,1,1024]{2,1,0:T(2,128)(2,1)} %get-tuple-element.23) | copy-start | bytes 1376260
  869.4 18.9 %copy-start.1 = (bf16[224,1,1024]{2,1,0:T(2,128)(2,1)S(1)}, bf16[224,1,1024]{2,1,0:T(2,128)(2,1)}, u32[]{:S(2)}) copy-start(bf16[224,1,1024]{2,1,0:T(2,128)(2,1)} %get-tuple-element.22) | copy-start | bytes 1376260
  869.5 19.9 %copy-start = (bf16[224,1,1024]{2,1,0:T(2,128)(2,1)S(1)}, bf16[224,1,1024]{2,1,0:T(2,128)(2,1)}, u32[]{:S(2)}) copy-start(bf16[224,1,1024]{2,1,0:T(2,128)(2,1)} %get-tuple-element.21) | copy-start | bytes 1376260
  871.7 37.6 %collective-permute-start = (bf16[224,1024]{1,0:T(8,128)(2,1)}, bf16[224,1024]{1,0:T(8,128)(2,1)}, u32[]{:S(2)}, u32[]{:S(2)}) collective-permute-start(bf16[224,1024]{1,0:T(8,128)(2,1)} %bitcast.100), channel_id=1, source_target_pairs={{0,1},{1,0},{2,3},{3,2},{4,5},{5,4},{6,7},{7,6},{8,9},{9,8},{10,11... | collective-permute-start | bytes 1376264 | tf_op jit(solution)/shard_map/ppermute | solution.py:71
  873.9 37.3 %collective-permute-start.1 = (bf16[224,1024]{1,0:T(8,128)(2,1)}, bf16[224,1024]{1,0:T(8,128)(2,1)}, u32[]{:S(2)}, u32[]{:S(2)}) collective-permute-start(bf16[224,1024]{1,0:T(8,128)(2,1)} %bitcast.99), channel_id=1, source_target_pairs={{0,2},{1,3},{2,0},{3,1},{4,6},{5,7},{6,4},{7,5},{8,10},{9,11},{10,... | collective-permute-start | bytes 1376264 | tf_op jit(solution)/shard_map/ppermute | solution.py:71
  876.0 39.7 %collective-permute-start.2 = (bf16[224,1024]{1,0:T(8,128)(2,1)}, bf16[224,1024]{1,0:T(8,128)(2,1)}, u32[]{:S(2)}, u32[]{:S(2)}) collective-permute-start(bf16[224,1024]{1,0:T(8,128)(2,1)} %bitcast.98), channel_id=1, source_target_pairs={{0,3},{1,2},{2,1},{3,0},{4,7},{5,6},{6,5},{7,4},{8,11},{9,10},{10,... | collective-permute-start | bytes 1376264 | tf_op jit(solution)/shard_map/ppermute | solution.py:71
  880.0 37.6 %collective-permute-start.3 = (bf16[224,1024]{1,0:T(8,128)(2,1)}, bf16[224,1024]{1,0:T(8,128)(2,1)}, u32[]{:S(2)}, u32[]{:S(2)}) collective-permute-start(bf16[224,1024]{1,0:T(8,128)(2,1)} %bitcast.97), channel_id=1, source_target_pairs={{0,4},{1,5},{2,6},{3,7},{4,0},{5,1},{6,2},{7,3},{8,12},{9,13},{10,... | collective-permute-start | bytes 1376264 | tf_op jit(solution)/shard_map/ppermute | solution.py:71
  882.1 39.8 %collective-permute-start.4 = (bf16[224,1024]{1,0:T(8,128)(2,1)}, bf16[224,1024]{1,0:T(8,128)(2,1)S(1)}, u32[]{:S(2)}, u32[]{:S(2)}) collective-permute-start(bf16[224,1024]{1,0:T(8,128)(2,1)} %bitcast.96), channel_id=1, source_target_pairs={{0,5},{1,4},{2,7},{3,6},{4,1},{5,0},{6,3},{7,2},{8,13},{9,12},{10,... | collective-permute-start | bytes 1376264 | tf_op jit(solution)/shard_map/ppermute | solution.py:71
  908.4 75.9 %copy-start.8 = (bf16[224,1,1024]{2,0,1:T(8,128)(2,1)S(1)}, bf16[224,1,1024]{2,0,1:T(8,128)(2,1)}, u32[]{:S(2)}) copy-start(bf16[224,1,1024]{2,0,1:T(8,128)(2,1)} %copy.103) | copy-start | bytes 1376260
  908.4 89.4 %copy-start.7 = (bf16[224,1,1024]{2,0,1:T(8,128)(2,1)S(1)}, bf16[224,1,1024]{2,0,1:T(8,128)(2,1)}, u32[]{:S(2)}) copy-start(bf16[224,1,1024]{2,0,1:T(8,128)(2,1)} %copy.102) | copy-start | bytes 1376260
  909.3 25.1 %collective-permute-start.5 = (bf16[224,1024]{1,0:T(8,128)(2,1)}, bf16[224,1024]{1,0:T(8,128)(2,1)S(1)}, u32[]{:S(2)}, u32[]{:S(2)}) collective-permute-start(bf16[224,1024]{1,0:T(8,128)(2,1)} %bitcast.95), channel_id=1, source_target_pairs={{0,6},{1,7},{2,4},{3,5},{4,2},{5,3},{6,0},{7,1},{8,14},{9,15},{10,... | collective-permute-start | bytes 1376264 | tf_op jit(solution)/shard_map/ppermute | solution.py:71
  911.2 32.2 %collective-permute-start.6 = (bf16[224,1024]{1,0:T(8,128)(2,1)}, bf16[224,1024]{1,0:T(8,128)(2,1)S(1)}, u32[]{:S(2)}, u32[]{:S(2)}) collective-permute-start(bf16[224,1024]{1,0:T(8,128)(2,1)} %bitcast.94), channel_id=1, source_target_pairs={{0,7},{1,6},{2,5},{3,4},{4,3},{5,2},{6,1},{7,0},{8,15},{9,14},{10,... | collective-permute-start | bytes 1376264 | tf_op jit(solution)/shard_map/ppermute | solution.py:71
  915.7 68.6 %collective-permute-start.7 = (bf16[224,1024]{1,0:T(8,128)(2,1)}, bf16[224,1024]{1,0:T(8,128)(2,1)S(1)}, u32[]{:S(2)}, u32[]{:S(2)}) collective-permute-start(bf16[224,1024]{1,0:T(8,128)(2,1)} %bitcast.93), channel_id=1, source_target_pairs={{0,8},{1,9},{2,10},{3,11},{4,12},{5,13},{6,14},{7,15},{8,0},{9,1},... | collective-permute-start | bytes 1376264 | tf_op jit(solution)/shard_map/ppermute | solution.py:71
  917.5 80.2 %collective-permute-start.8 = (bf16[224,1024]{1,0:T(8,128)(2,1)}, bf16[224,1024]{1,0:T(8,128)(2,1)S(1)}, u32[]{:S(2)}, u32[]{:S(2)}) collective-permute-start(bf16[224,1024]{1,0:T(8,128)(2,1)} %bitcast.92), channel_id=1, source_target_pairs={{0,9},{1,8},{2,11},{3,10},{4,13},{5,12},{6,15},{7,14},{8,1},{9,0},... | collective-permute-start | bytes 1376264 | tf_op jit(solution)/shard_map/ppermute | solution.py:71
  921.9 96.6 %collective-permute-start.9 = (bf16[224,1024]{1,0:T(8,128)(2,1)}, bf16[224,1024]{1,0:T(8,128)(2,1)S(1)}, u32[]{:S(2)}, u32[]{:S(2)}) collective-permute-start(bf16[224,1024]{1,0:T(8,128)(2,1)} %bitcast.113), channel_id=1, source_target_pairs={{0,10},{1,11},{2,8},{3,9},{4,14},{5,15},{6,12},{7,13},{8,2},{9,3},... | collective-permute-start | bytes 1376264 | tf_op jit(solution)/shard_map/ppermute | solution.py:71
  934.4 102.0 %collective-permute-start.10 = (bf16[224,1024]{1,0:T(8,128)(2,1)}, bf16[224,1024]{1,0:T(8,128)(2,1)S(1)}, u32[]{:S(2)}, u32[]{:S(2)}) collective-permute-start(bf16[224,1024]{1,0:T(8,128)(2,1)} %bitcast.112), channel_id=1, source_target_pairs={{0,11},{1,10},{2,9},{3,8},{4,15},{5,14},{6,13},{7,12},{8,3},{9,2},... | collective-permute-start | bytes 1376264 | tf_op jit(solution)/shard_map/ppermute | solution.py:71
  943.5 93.8 %collective-permute-start.11 = (bf16[224,1024]{1,0:T(8,128)(2,1)}, bf16[224,1024]{1,0:T(8,128)(2,1)S(1)}, u32[]{:S(2)}, u32[]{:S(2)}) collective-permute-start(bf16[224,1024]{1,0:T(8,128)(2,1)} %bitcast.111), channel_id=1, source_target_pairs={{0,12},{1,13},{2,14},{3,15},{4,8},{5,9},{6,10},{7,11},{8,4},{9,5},... | collective-permute-start | bytes 1376264 | tf_op jit(solution)/shard_map/ppermute | solution.py:71
  984.3 53.8 %collective-permute-start.12 = (bf16[224,1024]{1,0:T(8,128)(2,1)S(1)}, bf16[224,1024]{1,0:T(8,128)(2,1)S(1)}, u32[]{:S(2)}, u32[]{:S(2)}) collective-permute-start(bf16[224,1024]{1,0:T(8,128)(2,1)S(1)} %bitcast.110), channel_id=1, source_target_pairs={{0,13},{1,12},{2,15},{3,14},{4,9},{5,8},{6,11},{7,10},{8,5},{9,4},... | collective-permute-start | bytes 1376264 | tf_op jit(solution)/shard_map/ppermute | solution.py:71
  997.8 41.1 %collective-permute-start.13 = (bf16[224,1024]{1,0:T(8,128)(2,1)S(1)}, bf16[224,1024]{1,0:T(8,128)(2,1)S(1)}, u32[]{:S(2)}, u32[]{:S(2)}) collective-permute-start(bf16[224,1024]{1,0:T(8,128)(2,1)S(1)} %bitcast.109), channel_id=1, source_target_pairs={{0,14},{1,15},{2,12},{3,13},{4,10},{5,11},{6,8},{7,9},{8,6},{9,7},... | collective-permute-start | bytes 1376264 | tf_op jit(solution)/shard_map/ppermute | solution.py:71
  1018.5 21.2 %collective-permute-start.14 = (bf16[224,1024]{1,0:T(8,128)(2,1)S(1)}, bf16[224,1024]{1,0:T(8,128)(2,1)S(1)}, u32[]{:S(2)}, u32[]{:S(2)}) collective-permute-start(bf16[224,1024]{1,0:T(8,128)(2,1)S(1)} %bitcast.108), channel_id=1, source_target_pairs={{0,15},{1,14},{2,13},{3,12},{4,11},{5,10},{6,9},{7,8},{8,7},{9,6},... | collective-permute-start | bytes 1376264 | tf_op jit(solution)/shard_map/ppermute | solution.py:71
Sparse Core Ops, SparseCore 0:
  16.7 180.6 all-gather.2
  220.6 76.7 reduce-scatter.4
  300.1 81.2 all-gather.4
  443.5 206.3 reduce-scatter.6
